TPU v7x, 512 devices: a whole 4x4x16 slice. The times are simulated.
512 devices in a mesh: freq: 64 (over z_lo, x, core), lat: 8 (over z_hi, y).
Axes of the slice: x: 4, y: 4, z: 16 (z_hi: 2, z_lo: 8; z = z_hi * 8 + z_lo), core: 2. Of those that a mesh axis runs over, the one named last changes fastest.
Arguments:
- frequencies: float32 [64], P('freq'), may hold values from 0.3 to 1.5
- slowness: float32 [2, 128, 1024], P(None, 'lat', 'freq'), may hold values from 0.5 to 1.5
- src_field: float32 [64, 2, 128, 1024], P('freq', None, 'lat'), may hold values from -6 to 6
- rec_field: float32 [64, 2, 128, 1024], P('freq', None, 'lat'), may hold values from -6 to 6
Outputs:
- depth_image: float32 [2, 128, 1024], P(None, 'lat', 'freq')
- src_final: float32 [64, 2, 128, 1024], P('freq', None, 'lat')
- rec_final: float32 [64, 2, 128, 1024], P('freq', None, 'lat')
All inputs are finite; a program needn't handle non-finite values.
Results may differ from a plain program's by a relative error of at most 0.0003.
Values sent between devices are 32-bit elements; how exact they have to be, the bound alone decides.
A program may use at most 64 MiB of HBM per device.

v0:
```python
import math
import jax
import jax.numpy as jnp
from jax import lax
from jax.sharding import PartitionSpec as P

NZ = 2
TERMS = 8
step_ratio = 1.0
damping = 0.1


def extended(block, sides, width):
    for axis, dim in sides:
        count = lax.axis_size(axis)
        forward = [(i, i + 1) for i in range(count - 1)]
        backward = [(target, source) for source, target in forward]
        low = lax.ppermute(
            lax.slice_in_dim(block, block.shape[dim] - width, None, axis=dim), axis, forward
        )
        high = lax.ppermute(lax.slice_in_dim(block, 0, width, axis=dim), axis, backward)
        block = jnp.concatenate([low, block, high], axis=dim)
    return block


def neighbours(values):
    zero_col = jnp.zeros_like(values[..., :1])
    from_right = jnp.concatenate([values[..., 1:], zero_col], axis=-1)
    from_left = jnp.concatenate([zero_col, values[..., :-1]], axis=-1)
    return from_right + from_left


def mcclellan(padded):
    centre = padded[..., 1:-1, :]
    vertical = padded[..., 2:, :] + padded[..., :-2, :]
    return -0.5 * centre + 0.25 * vertical + neighbours(0.25 * centre + 0.125 * vertical)


def coefficients(wavenum, term_count):
    angles = math.pi * (jnp.arange(term_count, dtype=jnp.float32) + 0.5) / term_count
    view_shape = (term_count,) + (1,) * wavenum.ndim
    node_angles = angles.reshape(view_shape)
    excess = wavenum[None] ** 2 - node_angles**2
    absorb = damping * wavenum[None] ** 2
    modulus = jnp.sqrt(excess * excess + absorb * absorb)
    larger = jnp.sqrt(0.5 * (modulus + jnp.abs(excess)))
    smaller = absorb / (2.0 * larger)
    propagating = excess >= 0
    real_part = jnp.where(propagating, larger, smaller)
    imag_part = jnp.where(propagating, smaller, larger)
    attenuation = jnp.exp(-step_ratio * imag_part)
    phase_re = attenuation * jnp.cos(step_ratio * real_part)
    phase_im = attenuation * jnp.sin(step_ratio * real_part)
    orders = jnp.arange(term_count, dtype=jnp.float32)
    weights = jnp.where(orders == 0, 1.0, 2.0) / term_count
    cosine_table = weights[:, None] * jnp.cos(orders[:, None] * angles[None, :])
    coef_re = jnp.einsum("nj,j...->n...", cosine_table, phase_re, precision=lax.Precision.HIGHEST)
    coef_im = jnp.einsum("nj,j...->n...", cosine_table, phase_im, precision=lax.Precision.HIGHEST)
    return (coef_re, coef_im)


def accumulate(summed, coef_re, coef_im, level):
    src_re = level[..., 0, :, :]
    src_im = level[..., 1, :, :]
    rec_re = level[..., 2, :, :]
    rec_im = level[..., 3, :, :]
    term = jnp.stack(
        [
            coef_re * src_re - coef_im * src_im,
            coef_re * src_im + coef_im * src_re,
            coef_re * rec_re + coef_im * rec_im,
            coef_re * rec_im - coef_im * rec_re,
        ],
        axis=-3,
    )
    return summed + term


def raise_level(values):
    padded = extended(values, (("lat", 2),), 1)
    return mcclellan(padded)


def rim_step(wavefields, coef_re, coef_im):
    term_count = coef_re.shape[0]
    previous = wavefields
    summed = accumulate(jnp.zeros_like(wavefields), coef_re[0], coef_im[0], previous)
    current = raise_level(previous)
    summed = accumulate(summed, coef_re[1], coef_im[1], current)
    for term_index in range(2, term_count):
        following = 2.0 * raise_level(current) - previous
        summed = accumulate(summed, coef_re[term_index], coef_im[term_index], following)
        previous, current = (current, following)
    return summed


def shards(frequencies, slowness, src_field, rec_field):
    wavefields = jnp.concatenate([src_field, rec_field], axis=1)
    freq_count = lax.axis_size("freq")
    norm_factor = 1.0 / math.sqrt(wavefields.shape[0] * freq_count)
    full_slow = lax.all_gather(slowness, "freq", axis=2, tiled=True)
    partials = []
    for depth_step in range(NZ):
        slow_layer = full_slow[depth_step]
        coef_re, coef_im = coefficients(frequencies[:, None, None] * slow_layer[None], TERMS)
        wavefields = rim_step(wavefields, coef_re, coef_im)
        partial_value = jnp.sum(
            wavefields[:, 0] * wavefields[:, 2] + wavefields[:, 1] * wavefields[:, 3], axis=0
        )
        partials.append(partial_value)
    depth_image = (
        lax.psum_scatter(jnp.stack(partials), "freq", scatter_dimension=2, tiled=True) * norm_factor
    )
    return (depth_image, wavefields[:, :2], wavefields[:, 2:])


def solution(mesh):
    placed = (
        P("freq"),
        P(None, "lat", "freq"),
        P("freq", None, "lat", None),
        P("freq", None, "lat", None),
    )
    return jax.shard_map(
        shards,
        mesh=mesh,
        in_specs=placed,
        out_specs=(
            P(None, "lat", "freq"),
            P("freq", None, "lat", None),
            P("freq", None, "lat", None),
        ),
        check_vma=False,
    )
```

profile of v0, /device:TPU:8, one launch (start us, length us, event | category | flops | bytes accessed | tf_op | source)
XLA Modules:
  0.0 897.7 jit_solution(5849739694801983435)
XLA Ops:
  7.2 1.1 fusion.124
  8.3 1.1 fusion.125
  9.5 7.7 collective-permute-start
  17.2 1.9 collective-permute-start.1
  20.6 124.5 %all_gather.3 = f32[2,16,1024]{1,0,2:T(2,128)S(1)} all-gather(f32[2,16,16]{1,0,2:T(2,128)S(1)} %copy.34), channel_id=1, replica_groups=mesh['freq'=64,'lat'=8] {'freq'}, dimensions={2}, use_global_device_ids=true | all-gather | bytes 133120 | tf_op jit(solution)/shard_map/all_gather | solution.py:101
  146.6 2.8 fusion.27
  149.4 2.8 fusion.24
  152.3 2.8 fusion.21
  155.3 2.8 fusion.18
  160.1 2.4 collective-permute-start.2
  162.5 3.5 collective-permute-start.3
  166.0 1.5 subtract_bitcast_fusion.29
  169.1 0.8 multiply_subtract_fusion.11
  169.9 1.9 collective-permute-start.4
  171.8 13.0 %collective-permute-start.5 = (f32[1,4,1,1024]{3,0,2,1:T(1,128)S(1)}, f32[1,4,1,1024]{3,0,2,1:T(1,128)S(1)}, u32[]{:S(2)}, u32[]{:S(2)}) collective-permute-start(f32[1,4,1,1024]{3,0,2,1:T(1,128)S(1)} %get-tuple-element.133), channel_id=1, source_target_pairs={{0,1},{1,2},{2,3},{3,4},{4,5},{5,6},{6,7},{8,9},{9,10},{10,11},{11... | collective-permute-start | bytes 49160 | tf_op jit(solution)/shard_map/ppermute | solution.py:18
  184.9 1.5 subtract_bitcast_fusion.27
  187.3 0.8 multiply_subtract_fusion.10
  188.2 1.9 collective-permute-start.6
  190.1 14.7 %collective-permute-start.7 = (f32[1,4,1,1024]{3,0,2,1:T(1,128)S(1)}, f32[1,4,1,1024]{3,0,2,1:T(1,128)S(1)}, u32[]{:S(2)}, u32[]{:S(2)}) collective-permute-start(f32[1,4,1,1024]{3,0,2,1:T(1,128)S(1)} %get-tuple-element.129), channel_id=1, source_target_pairs={{0,1},{1,2},{2,3},{3,4},{4,5},{5,6},{6,7},{8,9},{9,10},{10,11},{11... | collective-permute-start | bytes 49160 | tf_op jit(solution)/shard_map/ppermute | solution.py:18
  204.9 1.5 subtract_bitcast_fusion.25
  207.3 0.8 multiply_subtract_fusion.9
  208.2 1.9 collective-permute-start.8
  210.1 14.9 %collective-permute-start.9 = (f32[1,4,1,1024]{3,0,2,1:T(1,128)S(1)}, f32[1,4,1,1024]{3,0,2,1:T(1,128)S(1)}, u32[]{:S(2)}, u32[]{:S(2)}) collective-permute-start(f32[1,4,1,1024]{3,0,2,1:T(1,128)S(1)} %get-tuple-element.125), channel_id=1, source_target_pairs={{0,1},{1,2},{2,3},{3,4},{4,5},{5,6},{6,7},{8,9},{9,10},{10,11},{11... | collective-permute-start | bytes 49160 | tf_op jit(solution)/shard_map/ppermute | solution.py:18
  225.0 1.5 subtract_bitcast_fusion.23
  228.3 1.9 collective-permute-start.10
  230.2 15.3 %collective-permute-start.11 = (f32[1,4,1,1024]{3,0,2,1:T(1,128)S(1)}, f32[1,4,1,1024]{3,0,2,1:T(1,128)S(1)}, u32[]{:S(2)}, u32[]{:S(2)}) collective-permute-start(f32[1,4,1,1024]{3,0,2,1:T(1,128)S(1)} %get-tuple-element.121), channel_id=1, source_target_pairs={{0,1},{1,2},{2,3},{3,4},{4,5},{5,6},{6,7},{8,9},{9,10},{10,11},{11... | collective-permute-start | bytes 49160 | tf_op jit(solution)/shard_map/ppermute | solution.py:18
  245.6 1.5 subtract_bitcast_fusion.21
  248.1 0.8 multiply_subtract_fusion.7
  248.9 1.9 collective-permute-start.12
  250.8 14.9 %collective-permute-start.13 = (f32[1,4,1,1024]{3,0,2,1:T(1,128)S(1)}, f32[1,4,1,1024]{3,0,2,1:T(1,128)S(1)}, u32[]{:S(2)}, u32[]{:S(2)}) collective-permute-start(f32[1,4,1,1024]{3,0,2,1:T(1,128)S(1)} %get-tuple-element.117), channel_id=1, source_target_pairs={{0,1},{1,2},{2,3},{3,4},{4,5},{5,6},{6,7},{8,9},{9,10},{10,11},{11... | collective-permute-start | bytes 49160 | tf_op jit(solution)/shard_map/ppermute | solution.py:18
  265.8 1.5 subtract_bitcast_fusion.19
  268.3 0.8 multiply_subtract_fusion.6
  269.1 1.5 subtract_bitcast_fusion.17
  270.6 1.5 maximum_add_fusion.2
  272.0 1.9 collective-permute-start.14
  274.0 14.9 %collective-permute-start.15 = (f32[1,4,1,1024]{3,0,2,1:T(1,128)S(1)}, f32[1,4,1,1024]{3,0,2,1:T(1,128)S(1)}, u32[]{:S(2)}, u32[]{:S(2)}) collective-permute-start(f32[1,4,1,1024]{3,0,2,1:T(1,128)S(1)} %get-tuple-element.113), channel_id=1, source_target_pairs={{0,1},{1,2},{2,3},{3,4},{4,5},{5,6},{6,7},{8,9},{9,10},{10,11},{11... | collective-permute-start | bytes 49160 | tf_op jit(solution)/shard_map/ppermute | solution.py:18
  289.3 1.1 collective-permute-done.15
  292.0 1.9 collective-permute-start.16
  294.0 14.7 %collective-permute-start.17 = (f32[1,4,1,1024]{3,0,2,1:T(1,128)S(1)}, f32[1,4,1,1024]{3,0,2,1:T(1,128)S(1)}, u32[]{:S(2)}, u32[]{:S(2)}) collective-permute-start(f32[1,4,1,1024]{3,0,2,1:T(1,128)S(1)} %get-tuple-element.109), channel_id=1, source_target_pairs={{0,1},{1,2},{2,3},{3,4},{4,5},{5,6},{6,7},{8,9},{9,10},{10,11},{11... | collective-permute-start | bytes 49160 | tf_op jit(solution)/shard_map/ppermute | solution.py:18
  309.0 1.1 collective-permute-done.17
  311.1 3.3 multiply_subtract_fusion.5
  314.4 1.9 collective-permute-start.18
  316.3 14.9 %collective-permute-start.19 = (f32[1,4,1,1024]{3,0,2,1:T(1,128)S(1)}, f32[1,4,1,1024]{3,0,2,1:T(1,128)S(1)}, u32[]{:S(2)}, u32[]{:S(2)}) collective-permute-start(f32[1,4,1,1024]{3,0,2,1:T(1,128)S(1)} %get-tuple-element.105), channel_id=1, source_target_pairs={{0,1},{1,2},{2,3},{3,4},{4,5},{5,6},{6,7},{8,9},{9,10},{10,11},{11... | collective-permute-start | bytes 49160 | tf_op jit(solution)/shard_map/ppermute | solution.py:18
  331.6 1.1 collective-permute-done.19
  333.7 0.8 multiply_subtract_fusion.4
  334.5 1.9 collective-permute-start.20
  336.4 15.2 %collective-permute-start.21 = (f32[1,4,1,1024]{3,0,2,1:T(1,128)S(1)}, f32[1,4,1,1024]{3,0,2,1:T(1,128)S(1)}, u32[]{:S(2)}, u32[]{:S(2)}) collective-permute-start(f32[1,4,1,1024]{3,0,2,1:T(1,128)S(1)} %get-tuple-element.101), channel_id=1, source_target_pairs={{0,1},{1,2},{2,3},{3,4},{4,5},{5,6},{6,7},{8,9},{9,10},{10,11},{11... | collective-permute-start | bytes 49160 | tf_op jit(solution)/shard_map/ppermute | solution.py:18
  351.9 1.0 collective-permute-done.21
  353.9 0.8 multiply_subtract_fusion.3
  354.7 1.9 collective-permute-start.22
  356.6 15.0 %collective-permute-start.23 = (f32[1,4,1,1024]{3,0,2,1:T(1,128)S(1)}, f32[1,4,1,1024]{3,0,2,1:T(1,128)S(1)}, u32[]{:S(2)}, u32[]{:S(2)}) collective-permute-start(f32[1,4,1,1024]{3,0,2,1:T(1,128)S(1)} %get-tuple-element.97), channel_id=1, source_target_pairs={{0,1},{1,2},{2,3},{3,4},{4,5},{5,6},{6,7},{8,9},{9,10},{10,11},{11... | collective-permute-start | bytes 49160 | tf_op jit(solution)/shard_map/ppermute | solution.py:18
  372.0 1.1 collective-permute-done.23
  374.0 0.8 multiply_subtract_fusion.2
  374.9 1.9 collective-permute-start.24
  376.8 15.0 %collective-permute-start.25 = (f32[1,4,1,1024]{3,0,2,1:T(1,128)S(1)}, f32[1,4,1,1024]{3,0,2,1:T(1,128)S(1)}, u32[]{:S(2)}, u32[]{:S(2)}) collective-permute-start(f32[1,4,1,1024]{3,0,2,1:T(1,128)S(1)} %get-tuple-element.93), channel_id=1, source_target_pairs={{0,1},{1,2},{2,3},{3,4},{4,5},{5,6},{6,7},{8,9},{9,10},{10,11},{11... | collective-permute-start | bytes 49160 | tf_op jit(solution)/shard_map/ppermute | solution.py:18
  392.1 1.1 collective-permute-done.25
  394.2 0.8 multiply_subtract_fusion.1
  395.1 1.9 collective-permute-start.26
  397.0 15.0 %collective-permute-start.27 = (f32[1,4,1,1024]{3,0,2,1:T(1,128)S(1)}, f32[1,4,1,1024]{3,0,2,1:T(1,128)S(1)}, u32[]{:S(2)}, u32[]{:S(2)}) collective-permute-start(f32[1,4,1,1024]{3,0,2,1:T(1,128)S(1)} %get-tuple-element.89), channel_id=1, source_target_pairs={{0,1},{1,2},{2,3},{3,4},{4,5},{5,6},{6,7},{8,9},{9,10},{10,11},{11... | collective-permute-start | bytes 49160 | tf_op jit(solution)/shard_map/ppermute | solution.py:18
  412.3 1.1 collective-permute-done.27
  415.5 1.5 maximum_add_fusion.5
  417.2 5.9 copy.46
  423.2 7.1 reshape.1693
  431.6 457.5 %reduce-scatter.4.cloned.1.call-done = f32[16,32]{1,0:T(8,128)} async-done(((f32[1024,32]{1,0:T(8,128)}), f32[16,32]{1,0:T(8,128)}) %reduce-scatter.4.cloned.1.call-update) | async-done | bytes 2064
  (101 shorter events, 25.6 us)
Async XLA Ops:
  7.2 881.9 %reduce-scatter.4.cloned.1.call-start = ((), (), s32[]{:S(2)}) async-start(), calls=%async_computation.1 | async-start | bytes 532480
  9.5 148.7 %collective-permute-start = (f32[1,4,1,1024]{3,0,2,1:T(1,128)S(1)}, f32[1,4,1,1024]{3,0,2,1:T(1,128)S(1)}, u32[]{:S(2)}, u32[]{:S(2)}) collective-permute-start(f32[1,4,1,1024]{3,0,2,1:T(1,128)S(1)} %get-tuple-element.140), channel_id=1, source_target_pairs={{1,0},{2,1},{3,2},{4,3},{5,4},{6,5},{7,6},{9,8},{10,9},{11,10},{12... | collective-permute-start | bytes 49160 | tf_op jit(solution)/shard_map/ppermute | solution.py:21
  17.2 140.9 %collective-permute-start.1 = (f32[1,4,1,1024]{3,0,2,1:T(1,128)S(1)}, f32[1,4,1,1024]{3,0,2,1:T(1,128)S(1)}, u32[]{:S(2)}, u32[]{:S(2)}) collective-permute-start(f32[1,4,1,1024]{3,0,2,1:T(1,128)S(1)} %get-tuple-element.141), channel_id=1, source_target_pairs={{0,1},{1,2},{2,3},{3,4},{4,5},{5,6},{6,7},{8,9},{9,10},{10,11},{11... | collective-permute-start | bytes 49160 | tf_op jit(solution)/shard_map/ppermute | solution.py:18
  149.4 16.5 %copy-start = (f32[8,16,1024]{2,0,1:T(8,128)}, f32[8,16,1024]{2,0,1:T(8,128)S(1)}, u32[]{:S(2)}) copy-start(f32[8,16,1024]{2,0,1:T(8,128)S(1)} %fusion.27) | copy-start | bytes 1572868
  152.3 13.7 %copy-start.1 = (f32[8,16,1024]{2,0,1:T(8,128)}, f32[8,16,1024]{2,0,1:T(8,128)S(1)}, u32[]{:S(2)}) copy-start(f32[8,16,1024]{2,0,1:T(8,128)S(1)} %fusion.24) | copy-start | bytes 1572868
  160.1 7.4 collective-permute-start.2
  162.5 5.6 collective-permute-start.3
  169.9 16.5 %collective-permute-start.4 = (f32[1,4,1,1024]{3,0,2,1:T(1,128)S(1)}, f32[1,4,1,1024]{3,0,2,1:T(1,128)S(1)}, u32[]{:S(2)}, u32[]{:S(2)}) collective-permute-start(f32[1,4,1,1024]{3,0,2,1:T(1,128)S(1)} %get-tuple-element.132), channel_id=1, source_target_pairs={{1,0},{2,1},{3,2},{4,3},{5,4},{6,5},{7,6},{9,8},{10,9},{11,10},{12... | collective-permute-start | bytes 49160 | tf_op jit(solution)/shard_map/ppermute | solution.py:21
  171.8 14.5 %collective-permute-start.5 = (f32[1,4,1,1024]{3,0,2,1:T(1,128)S(1)}, f32[1,4,1,1024]{3,0,2,1:T(1,128)S(1)}, u32[]{:S(2)}, u32[]{:S(2)}) collective-permute-start(f32[1,4,1,1024]{3,0,2,1:T(1,128)S(1)} %get-tuple-element.133), channel_id=1, source_target_pairs={{0,1},{1,2},{2,3},{3,4},{4,5},{5,6},{6,7},{8,9},{9,10},{10,11},{11... | collective-permute-start | bytes 49160 | tf_op jit(solution)/shard_map/ppermute | solution.py:18
  188.2 18.2 %collective-permute-start.6 = (f32[1,4,1,1024]{3,0,2,1:T(1,128)S(1)}, f32[1,4,1,1024]{3,0,2,1:T(1,128)S(1)}, u32[]{:S(2)}, u32[]{:S(2)}) collective-permute-start(f32[1,4,1,1024]{3,0,2,1:T(1,128)S(1)} %get-tuple-element.128), channel_id=1, source_target_pairs={{1,0},{2,1},{3,2},{4,3},{5,4},{6,5},{7,6},{9,8},{10,9},{11,10},{12... | collective-permute-start | bytes 49160 | tf_op jit(solution)/shard_map/ppermute | solution.py:21
  190.1 16.2 %collective-permute-start.7 = (f32[1,4,1,1024]{3,0,2,1:T(1,128)S(1)}, f32[1,4,1,1024]{3,0,2,1:T(1,128)S(1)}, u32[]{:S(2)}, u32[]{:S(2)}) collective-permute-start(f32[1,4,1,1024]{3,0,2,1:T(1,128)S(1)} %get-tuple-element.129), channel_id=1, source_target_pairs={{0,1},{1,2},{2,3},{3,4},{4,5},{5,6},{6,7},{8,9},{9,10},{10,11},{11... | collective-permute-start | bytes 49160 | tf_op jit(solution)/shard_map/ppermute | solution.py:18
  208.2 18.3 %collective-permute-start.8 = (f32[1,4,1,1024]{3,0,2,1:T(1,128)S(1)}, f32[1,4,1,1024]{3,0,2,1:T(1,128)S(1)}, u32[]{:S(2)}, u32[]{:S(2)}) collective-permute-start(f32[1,4,1,1024]{3,0,2,1:T(1,128)S(1)} %get-tuple-element.124), channel_id=1, source_target_pairs={{1,0},{2,1},{3,2},{4,3},{5,4},{6,5},{7,6},{9,8},{10,9},{11,10},{12... | collective-permute-start | bytes 49160 | tf_op jit(solution)/shard_map/ppermute | solution.py:21
  210.1 16.4 %collective-permute-start.9 = (f32[1,4,1,1024]{3,0,2,1:T(1,128)S(1)}, f32[1,4,1,1024]{3,0,2,1:T(1,128)S(1)}, u32[]{:S(2)}, u32[]{:S(2)}) collective-permute-start(f32[1,4,1,1024]{3,0,2,1:T(1,128)S(1)} %get-tuple-element.125), channel_id=1, source_target_pairs={{0,1},{1,2},{2,3},{3,4},{4,5},{5,6},{6,7},{8,9},{9,10},{10,11},{11... | collective-permute-start | bytes 49160 | tf_op jit(solution)/shard_map/ppermute | solution.py:18
  228.3 18.8 %collective-permute-start.10 = (f32[1,4,1,1024]{3,0,2,1:T(1,128)S(1)}, f32[1,4,1,1024]{3,0,2,1:T(1,128)S(1)}, u32[]{:S(2)}, u32[]{:S(2)}) collective-permute-start(f32[1,4,1,1024]{3,0,2,1:T(1,128)S(1)} %get-tuple-element.120), channel_id=1, source_target_pairs={{1,0},{2,1},{3,2},{4,3},{5,4},{6,5},{7,6},{9,8},{10,9},{11,10},{12... | collective-permute-start | bytes 49160 | tf_op jit(solution)/shard_map/ppermute | solution.py:21
  230.2 16.8 %collective-permute-start.11 = (f32[1,4,1,1024]{3,0,2,1:T(1,128)S(1)}, f32[1,4,1,1024]{3,0,2,1:T(1,128)S(1)}, u32[]{:S(2)}, u32[]{:S(2)}) collective-permute-start(f32[1,4,1,1024]{3,0,2,1:T(1,128)S(1)} %get-tuple-element.121), channel_id=1, source_target_pairs={{0,1},{1,2},{2,3},{3,4},{4,5},{5,6},{6,7},{8,9},{9,10},{10,11},{11... | collective-permute-start | bytes 49160 | tf_op jit(solution)/shard_map/ppermute | solution.py:18
  248.9 18.4 %collective-permute-start.12 = (f32[1,4,1,1024]{3,0,2,1:T(1,128)S(1)}, f32[1,4,1,1024]{3,0,2,1:T(1,128)S(1)}, u32[]{:S(2)}, u32[]{:S(2)}) collective-permute-start(f32[1,4,1,1024]{3,0,2,1:T(1,128)S(1)} %get-tuple-element.116), channel_id=1, source_target_pairs={{1,0},{2,1},{3,2},{4,3},{5,4},{6,5},{7,6},{9,8},{10,9},{11,10},{12... | collective-permute-start | bytes 49160 | tf_op jit(solution)/shard_map/ppermute | solution.py:21
  250.8 16.4 %collective-permute-start.13 = (f32[1,4,1,1024]{3,0,2,1:T(1,128)S(1)}, f32[1,4,1,1024]{3,0,2,1:T(1,128)S(1)}, u32[]{:S(2)}, u32[]{:S(2)}) collective-permute-start(f32[1,4,1,1024]{3,0,2,1:T(1,128)S(1)} %get-tuple-element.117), channel_id=1, source_target_pairs={{0,1},{1,2},{2,3},{3,4},{4,5},{5,6},{6,7},{8,9},{9,10},{10,11},{11... | collective-permute-start | bytes 49160 | tf_op jit(solution)/shard_map/ppermute | solution.py:18
  272.0 17.2 %collective-permute-start.14 = (f32[1,4,1,1024]{3,0,2,1:T(1,128)S(1)}, f32[1,4,1,1024]{3,0,2,1:T(1,128)S(1)}, u32[]{:S(2)}, u32[]{:S(2)}) collective-permute-start(f32[1,4,1,1024]{3,0,2,1:T(1,128)S(1)} %get-tuple-element.112), channel_id=1, source_target_pairs={{1,0},{2,1},{3,2},{4,3},{5,4},{6,5},{7,6},{9,8},{10,9},{11,10},{12... | collective-permute-start | bytes 49160 | tf_op jit(solution)/shard_map/ppermute | solution.py:21
  274.0 16.4 %collective-permute-start.15 = (f32[1,4,1,1024]{3,0,2,1:T(1,128)S(1)}, f32[1,4,1,1024]{3,0,2,1:T(1,128)S(1)}, u32[]{:S(2)}, u32[]{:S(2)}) collective-permute-start(f32[1,4,1,1024]{3,0,2,1:T(1,128)S(1)} %get-tuple-element.113), channel_id=1, source_target_pairs={{0,1},{1,2},{2,3},{3,4},{4,5},{5,6},{6,7},{8,9},{9,10},{10,11},{11... | collective-permute-start | bytes 49160 | tf_op jit(solution)/shard_map/ppermute | solution.py:18
  292.0 17.0 %collective-permute-start.16 = (f32[1,4,1,1024]{3,0,2,1:T(1,128)S(1)}, f32[1,4,1,1024]{3,0,2,1:T(1,128)S(1)}, u32[]{:S(2)}, u32[]{:S(2)}) collective-permute-start(f32[1,4,1,1024]{3,0,2,1:T(1,128)S(1)} %get-tuple-element.108), channel_id=1, source_target_pairs={{1,0},{2,1},{3,2},{4,3},{5,4},{6,5},{7,6},{9,8},{10,9},{11,10},{12... | collective-permute-start | bytes 49160 | tf_op jit(solution)/shard_map/ppermute | solution.py:21
  294.0 16.2 %collective-permute-start.17 = (f32[1,4,1,1024]{3,0,2,1:T(1,128)S(1)}, f32[1,4,1,1024]{3,0,2,1:T(1,128)S(1)}, u32[]{:S(2)}, u32[]{:S(2)}) collective-permute-start(f32[1,4,1,1024]{3,0,2,1:T(1,128)S(1)} %get-tuple-element.109), channel_id=1, source_target_pairs={{0,1},{1,2},{2,3},{3,4},{4,5},{5,6},{6,7},{8,9},{9,10},{10,11},{11... | collective-permute-start | bytes 49160 | tf_op jit(solution)/shard_map/ppermute | solution.py:18
  314.4 17.2 %collective-permute-start.18 = (f32[1,4,1,1024]{3,0,2,1:T(1,128)S(1)}, f32[1,4,1,1024]{3,0,2,1:T(1,128)S(1)}, u32[]{:S(2)}, u32[]{:S(2)}) collective-permute-start(f32[1,4,1,1024]{3,0,2,1:T(1,128)S(1)} %get-tuple-element.104), channel_id=1, source_target_pairs={{1,0},{2,1},{3,2},{4,3},{5,4},{6,5},{7,6},{9,8},{10,9},{11,10},{12... | collective-permute-start | bytes 49160 | tf_op jit(solution)/shard_map/ppermute | solution.py:21
  316.3 16.4 %collective-permute-start.19 = (f32[1,4,1,1024]{3,0,2,1:T(1,128)S(1)}, f32[1,4,1,1024]{3,0,2,1:T(1,128)S(1)}, u32[]{:S(2)}, u32[]{:S(2)}) collective-permute-start(f32[1,4,1,1024]{3,0,2,1:T(1,128)S(1)} %get-tuple-element.105), channel_id=1, source_target_pairs={{0,1},{1,2},{2,3},{3,4},{4,5},{5,6},{6,7},{8,9},{9,10},{10,11},{11... | collective-permute-start | bytes 49160 | tf_op jit(solution)/shard_map/ppermute | solution.py:18
  334.5 17.4 %collective-permute-start.20 = (f32[1,4,1,1024]{3,0,2,1:T(1,128)S(1)}, f32[1,4,1,1024]{3,0,2,1:T(1,128)S(1)}, u32[]{:S(2)}, u32[]{:S(2)}) collective-permute-start(f32[1,4,1,1024]{3,0,2,1:T(1,128)S(1)} %get-tuple-element.100), channel_id=1, source_target_pairs={{1,0},{2,1},{3,2},{4,3},{5,4},{6,5},{7,6},{9,8},{10,9},{11,10},{12... | collective-permute-start | bytes 49160 | tf_op jit(solution)/shard_map/ppermute | solution.py:21
  336.4 16.5 %collective-permute-start.21 = (f32[1,4,1,1024]{3,0,2,1:T(1,128)S(1)}, f32[1,4,1,1024]{3,0,2,1:T(1,128)S(1)}, u32[]{:S(2)}, u32[]{:S(2)}) collective-permute-start(f32[1,4,1,1024]{3,0,2,1:T(1,128)S(1)} %get-tuple-element.101), channel_id=1, source_target_pairs={{0,1},{1,2},{2,3},{3,4},{4,5},{5,6},{6,7},{8,9},{9,10},{10,11},{11... | collective-permute-start | bytes 49160 | tf_op jit(solution)/shard_map/ppermute | solution.py:18
  354.7 17.3 %collective-permute-start.22 = (f32[1,4,1,1024]{3,0,2,1:T(1,128)S(1)}, f32[1,4,1,1024]{3,0,2,1:T(1,128)S(1)}, u32[]{:S(2)}, u32[]{:S(2)}) collective-permute-start(f32[1,4,1,1024]{3,0,2,1:T(1,128)S(1)} %get-tuple-element.96), channel_id=1, source_target_pairs={{1,0},{2,1},{3,2},{4,3},{5,4},{6,5},{7,6},{9,8},{10,9},{11,10},{12... | collective-permute-start | bytes 49160 | tf_op jit(solution)/shard_map/ppermute | solution.py:21
  356.6 16.5 %collective-permute-start.23 = (f32[1,4,1,1024]{3,0,2,1:T(1,128)S(1)}, f32[1,4,1,1024]{3,0,2,1:T(1,128)S(1)}, u32[]{:S(2)}, u32[]{:S(2)}) collective-permute-start(f32[1,4,1,1024]{3,0,2,1:T(1,128)S(1)} %get-tuple-element.97), channel_id=1, source_target_pairs={{0,1},{1,2},{2,3},{3,4},{4,5},{5,6},{6,7},{8,9},{9,10},{10,11},{11... | collective-permute-start | bytes 49160 | tf_op jit(solution)/shard_map/ppermute | solution.py:18
  374.9 17.3 %collective-permute-start.24 = (f32[1,4,1,1024]{3,0,2,1:T(1,128)S(1)}, f32[1,4,1,1024]{3,0,2,1:T(1,128)S(1)}, u32[]{:S(2)}, u32[]{:S(2)}) collective-permute-start(f32[1,4,1,1024]{3,0,2,1:T(1,128)S(1)} %get-tuple-element.92), channel_id=1, source_target_pairs={{1,0},{2,1},{3,2},{4,3},{5,4},{6,5},{7,6},{9,8},{10,9},{11,10},{12... | collective-permute-start | bytes 49160 | tf_op jit(solution)/shard_map/ppermute | solution.py:21
  376.8 16.5 %collective-permute-start.25 = (f32[1,4,1,1024]{3,0,2,1:T(1,128)S(1)}, f32[1,4,1,1024]{3,0,2,1:T(1,128)S(1)}, u32[]{:S(2)}, u32[]{:S(2)}) collective-permute-start(f32[1,4,1,1024]{3,0,2,1:T(1,128)S(1)} %get-tuple-element.93), channel_id=1, source_target_pairs={{0,1},{1,2},{2,3},{3,4},{4,5},{5,6},{6,7},{8,9},{9,10},{10,11},{11... | collective-permute-start | bytes 49160 | tf_op jit(solution)/shard_map/ppermute | solution.py:18
  395.1 17.3 %collective-permute-start.26 = (f32[1,4,1,1024]{3,0,2,1:T(1,128)S(1)}, f32[1,4,1,1024]{3,0,2,1:T(1,128)S(1)}, u32[]{:S(2)}, u32[]{:S(2)}) collective-permute-start(f32[1,4,1,1024]{3,0,2,1:T(1,128)S(1)} %get-tuple-element.88), channel_id=1, source_target_pairs={{1,0},{2,1},{3,2},{4,3},{5,4},{6,5},{7,6},{9,8},{10,9},{11,10},{12... | collective-permute-start | bytes 49160 | tf_op jit(solution)/shard_map/ppermute | solution.py:21
  397.0 16.5 %collective-permute-start.27 = (f32[1,4,1,1024]{3,0,2,1:T(1,128)S(1)}, f32[1,4,1,1024]{3,0,2,1:T(1,128)S(1)}, u32[]{:S(2)}, u32[]{:S(2)}) collective-permute-start(f32[1,4,1,1024]{3,0,2,1:T(1,128)S(1)} %get-tuple-element.89), channel_id=1, source_target_pairs={{0,1},{1,2},{2,3},{3,4},{4,5},{5,6},{6,7},{8,9},{9,10},{10,11},{11... | collective-permute-start | bytes 49160 | tf_op jit(solution)/shard_map/ppermute | solution.py:18
Sparse Core Ops, SparseCore 0:
  430.4 458.6 reduce-scatter.3
where the time goes:
time: 901 us; the launch traced here: 898 us
  waiting for transfers between devices  466 us (52%)
  starting transfers between devices  216 us (24%)
  blocking collectives  124 us (14%)
  other arithmetic  34.9 us (4%)
  local copies, waits for them, and re-layouts  29 us (3%)
  between operations  15.8 us (2%)
  matrix products  11.2 us (1%)
    unnamed x2, waiting for transfers between devices  457 us
    ppermute x14, starting transfers between devices, extended(): lax.ppermute(lax.slice_in_dim(block, block.shape[dim] - width, None, axis...  183 us
    all_gather x1, blocking collectives, shards(): full_slow = lax.all_gather(slowness, 'freq', axis=2, tiled=True)  124 us
    ppermute x14, starting transfers between devices, extended(): lax.ppermute(lax.slice_in_dim(block, 0, width, axis=dim), axis, backward)  33.1 us
    unnamed x16, local copies, waits for them, and re-layouts  19.6 us
  transfers between devices with their start and end apart: 29, of which 9 were waited for; matrix products, arithmetic and copies ran while one was open for 3% of the time, Pallas kernels for 0%

commit v1 on v0

--- a/solution.py
+++ b/solution.py
@@ -98,7 +98,12 @@
     wavefields = jnp.concatenate([src_field, rec_field], axis=1)
     freq_count = lax.axis_size("freq")
     norm_factor = 1.0 / math.sqrt(wavefields.shape[0] * freq_count)
-    full_slow = lax.all_gather(slowness, "freq", axis=2, tiled=True)
+    full_slow = jnp.concatenate(
+        jax.lax.all_to_all(
+            jnp.stack([slowness for _ in range(jax.lax.axis_size("freq"))]), "freq", 0, 0
+        ),
+        axis=2,
+    )
     partials = []
     for depth_step in range(NZ):
         slow_layer = full_slow[depth_step]

time: 901 us -> 801 us (0.89)
  blocking collectives: 124 us -> 0 us
  waiting for transfers between devices: 466 us -> 478 us
  starting transfers between devices: 216 us -> 227 us
    all_gather x1 -> x0, blocking collectives: 124 us -> none  [shards(): full_slow = lax.all_gather(slowness, 'freq', axis=2, tiled=True)]
    all_to_all x0 -> x1, starting transfers between devices: none -> 15.4 us  [shards(): jax.lax.all_to_all(jnp.stack([slowness for _ in range(jax.lax.axis_size('...]
    ppermute x14, waiting for transfers between devices: 8.28 us -> 17.5 us  [extended(): lax.ppermute(lax.slice_in_dim(block, block.shape[dim] - width, None, axis...]
    unnamed x16 -> x15, local copies, waits for them, and re-layouts: 19.6 us -> 19.6 us
  transfers between devices with their start and end apart: 29 -> 30, of which waited for: 9 -> 14; matrix products, arithmetic and copies ran while one was open for 3% -> 1% of each run, Pallas kernels for 0% -> 0%
where the time goes in v1:
time: 801 us; the launch traced here: 791 us
  waiting for transfers between devices  478 us (60%)
  starting transfers between devices  227 us (28%)
  local copies, waits for them, and re-layouts  30.3 us (4%)
  other arithmetic  27.3 us (3%)
  between operations  15.8 us (2%)
  matrix products  12.4 us (2%)
    unnamed x2, waiting for transfers between devices  461 us
    ppermute x14, starting transfers between devices, extended(): lax.ppermute(lax.slice_in_dim(block, block.shape[dim] - width, None, axis...  179 us
    ppermute x14, starting transfers between devices, extended(): lax.ppermute(lax.slice_in_dim(block, 0, width, axis=dim), axis, backward)  32.7 us
    unnamed x15, local copies, waits for them, and re-layouts  19.6 us
    ppermute x14, waiting for transfers between devices, extended(): lax.ppermute(lax.slice_in_dim(block, block.shape[dim] - width, None, axis...  17.5 us
  transfers between devices with their start and end apart: 30, of which 14 were waited for; matrix products, arithmetic and copies ran while one was open for 1% of the time, Pallas kernels for 0%

profile of v1, /device:TPU:8, one launch (start us, length us, event | category | flops | bytes accessed | tf_op | source)
XLA Modules:
  0.0 791.3 jit_solution(13705648713179419107)
XLA Ops:
  7.2 1.1 fusion.125
  8.3 1.1 fusion.126
  9.4 7.7 collective-permute-start
  17.2 1.9 collective-permute-start.1
  19.1 3.7 collective-permute-done.1
  24.5 1.9 collective-permute-start.2
  26.4 3.9 collective-permute-start.3
  30.4 1.8 collective-permute-done.3
  33.1 0.8 multiply_subtract_fusion.11
  33.9 1.9 collective-permute-start.4
  35.9 7.8 collective-permute-start.5
  43.7 1.4 collective-permute-done.5
  46.0 0.8 multiply_subtract_fusion.10
  46.9 1.9 collective-permute-start.6
  48.8 15.0 %collective-permute-start.7 = (f32[1,4,1,1024]{3,0,2,1:T(1,128)S(1)}, f32[1,4,1,1024]{3,0,2,1:T(1,128)S(1)}, u32[]{:S(2)}, u32[]{:S(2)}) collective-permute-start(f32[1,4,1,1024]{3,0,2,1:T(1,128)S(1)} %get-tuple-element.128), channel_id=1, source_target_pairs={{0,1},{1,2},{2,3},{3,4},{4,5},{5,6},{6,7},{8,9},{9,10},{10,11},{11... | collective-permute-start | bytes 49160 | tf_op jit(solution)/shard_map/ppermute | solution.py:18
  63.8 1.4 collective-permute-done.7
  66.2 0.8 multiply_subtract_fusion.9
  67.1 1.9 collective-permute-start.8
  69.0 15.0 %collective-permute-start.9 = (f32[1,4,1,1024]{3,0,2,1:T(1,128)S(1)}, f32[1,4,1,1024]{3,0,2,1:T(1,128)S(1)}, u32[]{:S(2)}, u32[]{:S(2)}) collective-permute-start(f32[1,4,1,1024]{3,0,2,1:T(1,128)S(1)} %get-tuple-element.124), channel_id=1, source_target_pairs={{0,1},{1,2},{2,3},{3,4},{4,5},{5,6},{6,7},{8,9},{9,10},{10,11},{11... | collective-permute-start | bytes 49160 | tf_op jit(solution)/shard_map/ppermute | solution.py:18
  84.1 1.1 reshape.1718
  85.2 15.4 %all-to-all-start = ((f32[64,1,512]{2,1,0:T(1,128)}), f32[64,1,512]{2,1,0:T(1,128)S(1)}, u32[]{:S(2)}, u32[]{:S(2)}) async-start(f32[64,1,512]{2,1,0:T(1,128)} %reshape.1718), calls=%async_computation | async-start | bytes 262144 | tf_op jit(solution)/shard_map/all_to_all | solution.py:102
  101.6 0.8 multiply_subtract_fusion.8
  102.4 1.9 collective-permute-start.10
  104.4 15.2 %collective-permute-start.11 = (f32[1,4,1,1024]{3,0,2,1:T(1,128)S(1)}, f32[1,4,1,1024]{3,0,2,1:T(1,128)S(1)}, u32[]{:S(2)}, u32[]{:S(2)}) collective-permute-start(f32[1,4,1,1024]{3,0,2,1:T(1,128)S(1)} %get-tuple-element.120), channel_id=1, source_target_pairs={{0,1},{1,2},{2,3},{3,4},{4,5},{5,6},{6,7},{8,9},{9,10},{10,11},{11... | collective-permute-start | bytes 49160 | tf_op jit(solution)/shard_map/ppermute | solution.py:18
  119.6 1.2 collective-permute-done.11
  121.8 0.8 multiply_subtract_fusion.7
  122.6 1.9 collective-permute-start.12
  124.6 15.0 %collective-permute-start.13 = (f32[1,4,1,1024]{3,0,2,1:T(1,128)S(1)}, f32[1,4,1,1024]{3,0,2,1:T(1,128)S(1)}, u32[]{:S(2)}, u32[]{:S(2)}) collective-permute-start(f32[1,4,1,1024]{3,0,2,1:T(1,128)S(1)} %get-tuple-element.116), channel_id=1, source_target_pairs={{0,1},{1,2},{2,3},{3,4},{4,5},{5,6},{6,7},{8,9},{9,10},{10,11},{11... | collective-permute-start | bytes 49160 | tf_op jit(solution)/shard_map/ppermute | solution.py:18
  142.0 0.8 multiply_subtract_fusion.6
  143.3 0.9 reduce
  145.8 2.8 fusion.18
  148.6 4.0 fusion.21
  153.1 2.8 fusion.24
  155.9 2.8 fusion.27
  160.9 1.5 maximum_add_fusion.2
  162.4 1.9 collective-permute-start.14
  164.3 15.2 %collective-permute-start.15 = (f32[1,4,1,1024]{3,0,2,1:T(1,128)S(1)}, f32[1,4,1,1024]{3,0,2,1:T(1,128)S(1)}, u32[]{:S(2)}, u32[]{:S(2)}) collective-permute-start(f32[1,4,1,1024]{3,0,2,1:T(1,128)S(1)} %get-tuple-element.112), channel_id=1, source_target_pairs={{0,1},{1,2},{2,3},{3,4},{4,5},{5,6},{6,7},{8,9},{9,10},{10,11},{11... | collective-permute-start | bytes 49160 | tf_op jit(solution)/shard_map/ppermute | solution.py:18
  182.2 1.9 collective-permute-start.16
  184.1 15.0 %collective-permute-start.17 = (f32[1,4,1,1024]{3,0,2,1:T(1,128)S(1)}, f32[1,4,1,1024]{3,0,2,1:T(1,128)S(1)}, u32[]{:S(2)}, u32[]{:S(2)}) collective-permute-start(f32[1,4,1,1024]{3,0,2,1:T(1,128)S(1)} %get-tuple-element.108), channel_id=1, source_target_pairs={{0,1},{1,2},{2,3},{3,4},{4,5},{5,6},{6,7},{8,9},{9,10},{10,11},{11... | collective-permute-start | bytes 49160 | tf_op jit(solution)/shard_map/ppermute | solution.py:18
  199.5 1.1 collective-permute-done.17
  201.5 3.3 multiply_subtract_fusion.5
  204.9 1.9 collective-permute-start.18
  206.8 15.0 %collective-permute-start.19 = (f32[1,4,1,1024]{3,0,2,1:T(1,128)S(1)}, f32[1,4,1,1024]{3,0,2,1:T(1,128)S(1)}, u32[]{:S(2)}, u32[]{:S(2)}) collective-permute-start(f32[1,4,1,1024]{3,0,2,1:T(1,128)S(1)} %get-tuple-element.104), channel_id=1, source_target_pairs={{0,1},{1,2},{2,3},{3,4},{4,5},{5,6},{6,7},{8,9},{9,10},{10,11},{11... | collective-permute-start | bytes 49160 | tf_op jit(solution)/shard_map/ppermute | solution.py:18
  222.1 1.1 collective-permute-done.19
  224.2 0.8 multiply_subtract_fusion.4
  225.0 1.9 collective-permute-start.20
  227.0 15.0 %collective-permute-start.21 = (f32[1,4,1,1024]{3,0,2,1:T(1,128)S(1)}, f32[1,4,1,1024]{3,0,2,1:T(1,128)S(1)}, u32[]{:S(2)}, u32[]{:S(2)}) collective-permute-start(f32[1,4,1,1024]{3,0,2,1:T(1,128)S(1)} %get-tuple-element.100), channel_id=1, source_target_pairs={{0,1},{1,2},{2,3},{3,4},{4,5},{5,6},{6,7},{8,9},{9,10},{10,11},{11... | collective-permute-start | bytes 49160 | tf_op jit(solution)/shard_map/ppermute | solution.py:18
  242.3 1.1 collective-permute-done.21
  244.4 0.8 multiply_subtract_fusion.3
  245.2 1.9 collective-permute-start.22
  247.1 15.0 %collective-permute-start.23 = (f32[1,4,1,1024]{3,0,2,1:T(1,128)S(1)}, f32[1,4,1,1024]{3,0,2,1:T(1,128)S(1)}, u32[]{:S(2)}, u32[]{:S(2)}) collective-permute-start(f32[1,4,1,1024]{3,0,2,1:T(1,128)S(1)} %get-tuple-element.96), channel_id=1, source_target_pairs={{0,1},{1,2},{2,3},{3,4},{4,5},{5,6},{6,7},{8,9},{9,10},{10,11},{11... | collective-permute-start | bytes 49160 | tf_op jit(solution)/shard_map/ppermute | solution.py:18
  262.5 1.1 collective-permute-done.23
  264.6 0.8 multiply_subtract_fusion.2
  265.4 1.9 collective-permute-start.24
  267.3 15.2 %collective-permute-start.25 = (f32[1,4,1,1024]{3,0,2,1:T(1,128)S(1)}, f32[1,4,1,1024]{3,0,2,1:T(1,128)S(1)}, u32[]{:S(2)}, u32[]{:S(2)}) collective-permute-start(f32[1,4,1,1024]{3,0,2,1:T(1,128)S(1)} %get-tuple-element.92), channel_id=1, source_target_pairs={{0,1},{1,2},{2,3},{3,4},{4,5},{5,6},{6,7},{8,9},{9,10},{10,11},{11... | collective-permute-start | bytes 49160 | tf_op jit(solution)/shard_map/ppermute | solution.py:18
  282.8 1.0 collective-permute-done.25
  284.7 0.8 multiply_subtract_fusion.1
  285.6 1.9 collective-permute-start.26
  287.5 15.0 %collective-permute-start.27 = (f32[1,4,1,1024]{3,0,2,1:T(1,128)S(1)}, f32[1,4,1,1024]{3,0,2,1:T(1,128)S(1)}, u32[]{:S(2)}, u32[]{:S(2)}) collective-permute-start(f32[1,4,1,1024]{3,0,2,1:T(1,128)S(1)} %get-tuple-element.88), channel_id=1, source_target_pairs={{0,1},{1,2},{2,3},{3,4},{4,5},{5,6},{6,7},{8,9},{9,10},{10,11},{11... | collective-permute-start | bytes 49160 | tf_op jit(solution)/shard_map/ppermute | solution.py:18
  302.8 1.1 collective-permute-done.27
  306.0 1.5 maximum_add_fusion.5
  307.7 5.9 copy.48
  313.7 7.1 reshape.1716
  322.2 460.6 %reduce-scatter.4.cloned.1.call-done = f32[16,32]{1,0:T(8,128)} async-done(((f32[1024,32]{1,0:T(8,128)}), f32[16,32]{1,0:T(8,128)}) %reduce-scatter.4.cloned.1.call-update) | async-done | bytes 2064
  (108 shorter events, 27.5 us)
Async XLA Ops:
  7.2 76.9 %copy-start.1 = (f32[2,16,16]{2,1,0:T(8,128)S(1)}, f32[2,16,16]{2,1,0:T(8,128)}, u32[]{:S(2)}) copy-start(f32[2,16,16]{2,1,0:T(8,128)} %param.5) | copy-start | bytes 6148
  9.4 9.7 %collective-permute-start = (f32[1,4,1,1024]{3,0,2,1:T(1,128)S(1)}, f32[1,4,1,1024]{3,0,2,1:T(1,128)S(1)}, u32[]{:S(2)}, u32[]{:S(2)}) collective-permute-start(f32[1,4,1,1024]{3,0,2,1:T(1,128)S(1)} %get-tuple-element.139), channel_id=1, source_target_pairs={{1,0},{2,1},{3,2},{4,3},{5,4},{6,5},{7,6},{9,8},{10,9},{11,10},{12... | collective-permute-start | bytes 49160 | tf_op jit(solution)/shard_map/ppermute | solution.py:21
  17.2 5.6 collective-permute-start.1
  24.5 5.9 collective-permute-start.2
  26.4 5.7 collective-permute-start.3
  33.9 9.7 %collective-permute-start.4 = (f32[1,4,1,1024]{3,0,2,1:T(1,128)S(1)}, f32[1,4,1,1024]{3,0,2,1:T(1,128)S(1)}, u32[]{:S(2)}, u32[]{:S(2)}) collective-permute-start(f32[1,4,1,1024]{3,0,2,1:T(1,128)S(1)} %get-tuple-element.131), channel_id=1, source_target_pairs={{1,0},{2,1},{3,2},{4,3},{5,4},{6,5},{7,6},{9,8},{10,9},{11,10},{12... | collective-permute-start | bytes 49160 | tf_op jit(solution)/shard_map/ppermute | solution.py:21
  35.9 9.2 %collective-permute-start.5 = (f32[1,4,1,1024]{3,0,2,1:T(1,128)S(1)}, f32[1,4,1,1024]{3,0,2,1:T(1,128)S(1)}, u32[]{:S(2)}, u32[]{:S(2)}) collective-permute-start(f32[1,4,1,1024]{3,0,2,1:T(1,128)S(1)} %get-tuple-element.132), channel_id=1, source_target_pairs={{0,1},{1,2},{2,3},{3,4},{4,5},{5,6},{6,7},{8,9},{9,10},{10,11},{11... | collective-permute-start | bytes 49160 | tf_op jit(solution)/shard_map/ppermute | solution.py:18
  46.9 17.0 %collective-permute-start.6 = (f32[1,4,1,1024]{3,0,2,1:T(1,128)S(1)}, f32[1,4,1,1024]{3,0,2,1:T(1,128)S(1)}, u32[]{:S(2)}, u32[]{:S(2)}) collective-permute-start(f32[1,4,1,1024]{3,0,2,1:T(1,128)S(1)} %get-tuple-element.127), channel_id=1, source_target_pairs={{1,0},{2,1},{3,2},{4,3},{5,4},{6,5},{7,6},{9,8},{10,9},{11,10},{12... | collective-permute-start | bytes 49160 | tf_op jit(solution)/shard_map/ppermute | solution.py:21
  48.8 16.5 %collective-permute-start.7 = (f32[1,4,1,1024]{3,0,2,1:T(1,128)S(1)}, f32[1,4,1,1024]{3,0,2,1:T(1,128)S(1)}, u32[]{:S(2)}, u32[]{:S(2)}) collective-permute-start(f32[1,4,1,1024]{3,0,2,1:T(1,128)S(1)} %get-tuple-element.128), channel_id=1, source_target_pairs={{0,1},{1,2},{2,3},{3,4},{4,5},{5,6},{6,7},{8,9},{9,10},{10,11},{11... | collective-permute-start | bytes 49160 | tf_op jit(solution)/shard_map/ppermute | solution.py:18
  67.1 33.6 %collective-permute-start.8 = (f32[1,4,1,1024]{3,0,2,1:T(1,128)S(1)}, f32[1,4,1,1024]{3,0,2,1:T(1,128)S(1)}, u32[]{:S(2)}, u32[]{:S(2)}) collective-permute-start(f32[1,4,1,1024]{3,0,2,1:T(1,128)S(1)} %get-tuple-element.123), channel_id=1, source_target_pairs={{1,0},{2,1},{3,2},{4,3},{5,4},{6,5},{7,6},{9,8},{10,9},{11,10},{12... | collective-permute-start | bytes 49160 | tf_op jit(solution)/shard_map/ppermute | solution.py:21
  69.0 31.7 %collective-permute-start.9 = (f32[1,4,1,1024]{3,0,2,1:T(1,128)S(1)}, f32[1,4,1,1024]{3,0,2,1:T(1,128)S(1)}, u32[]{:S(2)}, u32[]{:S(2)}) collective-permute-start(f32[1,4,1,1024]{3,0,2,1:T(1,128)S(1)} %get-tuple-element.124), channel_id=1, source_target_pairs={{0,1},{1,2},{2,3},{3,4},{4,5},{5,6},{6,7},{8,9},{9,10},{10,11},{11... | collective-permute-start | bytes 49160 | tf_op jit(solution)/shard_map/ppermute | solution.py:18
  85.2 57.6 %all-to-all-start = ((f32[64,1,512]{2,1,0:T(1,128)}), f32[64,1,512]{2,1,0:T(1,128)S(1)}, u32[]{:S(2)}, u32[]{:S(2)}) async-start(f32[64,1,512]{2,1,0:T(1,128)} %reshape.1718), calls=%async_computation | async-start | bytes 262144 | tf_op jit(solution)/shard_map/all_to_all | solution.py:102
  100.6 682.1 %reduce-scatter.4.cloned.1.call-start = ((), (), s32[]{:S(2)}) async-start(), calls=%async_computation.2 | async-start | bytes 532480
  102.4 17.2 %collective-permute-start.10 = (f32[1,4,1,1024]{3,0,2,1:T(1,128)S(1)}, f32[1,4,1,1024]{3,0,2,1:T(1,128)S(1)}, u32[]{:S(2)}, u32[]{:S(2)}) collective-permute-start(f32[1,4,1,1024]{3,0,2,1:T(1,128)S(1)} %get-tuple-element.119), channel_id=1, source_target_pairs={{1,0},{2,1},{3,2},{4,3},{5,4},{6,5},{7,6},{9,8},{10,9},{11,10},{12... | collective-permute-start | bytes 49160 | tf_op jit(solution)/shard_map/ppermute | solution.py:21
  104.4 16.5 %collective-permute-start.11 = (f32[1,4,1,1024]{3,0,2,1:T(1,128)S(1)}, f32[1,4,1,1024]{3,0,2,1:T(1,128)S(1)}, u32[]{:S(2)}, u32[]{:S(2)}) collective-permute-start(f32[1,4,1,1024]{3,0,2,1:T(1,128)S(1)} %get-tuple-element.120), channel_id=1, source_target_pairs={{0,1},{1,2},{2,3},{3,4},{4,5},{5,6},{6,7},{8,9},{9,10},{10,11},{11... | collective-permute-start | bytes 49160 | tf_op jit(solution)/shard_map/ppermute | solution.py:18
  122.6 17.6 %collective-permute-start.12 = (f32[1,4,1,1024]{3,0,2,1:T(1,128)S(1)}, f32[1,4,1,1024]{3,0,2,1:T(1,128)S(1)}, u32[]{:S(2)}, u32[]{:S(2)}) collective-permute-start(f32[1,4,1,1024]{3,0,2,1:T(1,128)S(1)} %get-tuple-element.115), channel_id=1, source_target_pairs={{1,0},{2,1},{3,2},{4,3},{5,4},{6,5},{7,6},{9,8},{10,9},{11,10},{12... | collective-permute-start | bytes 49160 | tf_op jit(solution)/shard_map/ppermute | solution.py:21
  124.6 16.5 %collective-permute-start.13 = (f32[1,4,1,1024]{3,0,2,1:T(1,128)S(1)}, f32[1,4,1,1024]{3,0,2,1:T(1,128)S(1)}, u32[]{:S(2)}, u32[]{:S(2)}) collective-permute-start(f32[1,4,1,1024]{3,0,2,1:T(1,128)S(1)} %get-tuple-element.116), channel_id=1, source_target_pairs={{0,1},{1,2},{2,3},{3,4},{4,5},{5,6},{6,7},{8,9},{9,10},{10,11},{11... | collective-permute-start | bytes 49160 | tf_op jit(solution)/shard_map/ppermute | solution.py:18
  153.0 26.4 %copy-start = (f32[8,16,1024]{2,0,1:T(8,128)S(1)}, f32[8,16,1024]{2,0,1:T(8,128)}, u32[]{:S(2)}) copy-start(f32[8,16,1024]{2,0,1:T(8,128)} %fusion.21) | copy-start | bytes 1572868
  162.4 17.5 %collective-permute-start.14 = (f32[1,4,1,1024]{3,0,2,1:T(1,128)S(1)}, f32[1,4,1,1024]{3,0,2,1:T(1,128)S(1)}, u32[]{:S(2)}, u32[]{:S(2)}) collective-permute-start(f32[1,4,1,1024]{3,0,2,1:T(1,128)S(1)} %get-tuple-element.111), channel_id=1, source_target_pairs={{1,0},{2,1},{3,2},{4,3},{5,4},{6,5},{7,6},{9,8},{10,9},{11,10},{12... | collective-permute-start | bytes 49160 | tf_op jit(solution)/shard_map/ppermute | solution.py:21
  164.3 16.2 %collective-permute-start.15 = (f32[1,4,1,1024]{3,0,2,1:T(1,128)S(1)}, f32[1,4,1,1024]{3,0,2,1:T(1,128)S(1)}, u32[]{:S(2)}, u32[]{:S(2)}) collective-permute-start(f32[1,4,1,1024]{3,0,2,1:T(1,128)S(1)} %get-tuple-element.112), channel_id=1, source_target_pairs={{0,1},{1,2},{2,3},{3,4},{4,5},{5,6},{6,7},{8,9},{9,10},{10,11},{11... | collective-permute-start | bytes 49160 | tf_op jit(solution)/shard_map/ppermute | solution.py:18
  182.2 17.2 %collective-permute-start.16 = (f32[1,4,1,1024]{3,0,2,1:T(1,128)S(1)}, f32[1,4,1,1024]{3,0,2,1:T(1,128)S(1)}, u32[]{:S(2)}, u32[]{:S(2)}) collective-permute-start(f32[1,4,1,1024]{3,0,2,1:T(1,128)S(1)} %get-tuple-element.107), channel_id=1, source_target_pairs={{1,0},{2,1},{3,2},{4,3},{5,4},{6,5},{7,6},{9,8},{10,9},{11,10},{12... | collective-permute-start | bytes 49160 | tf_op jit(solution)/shard_map/ppermute | solution.py:21
  184.1 16.5 %collective-permute-start.17 = (f32[1,4,1,1024]{3,0,2,1:T(1,128)S(1)}, f32[1,4,1,1024]{3,0,2,1:T(1,128)S(1)}, u32[]{:S(2)}, u32[]{:S(2)}) collective-permute-start(f32[1,4,1,1024]{3,0,2,1:T(1,128)S(1)} %get-tuple-element.108), channel_id=1, source_target_pairs={{0,1},{1,2},{2,3},{3,4},{4,5},{5,6},{6,7},{8,9},{9,10},{10,11},{11... | collective-permute-start | bytes 49160 | tf_op jit(solution)/shard_map/ppermute | solution.py:18
  204.9 17.3 %collective-permute-start.18 = (f32[1,4,1,1024]{3,0,2,1:T(1,128)S(1)}, f32[1,4,1,1024]{3,0,2,1:T(1,128)S(1)}, u32[]{:S(2)}, u32[]{:S(2)}) collective-permute-start(f32[1,4,1,1024]{3,0,2,1:T(1,128)S(1)} %get-tuple-element.103), channel_id=1, source_target_pairs={{1,0},{2,1},{3,2},{4,3},{5,4},{6,5},{7,6},{9,8},{10,9},{11,10},{12... | collective-permute-start | bytes 49160 | tf_op jit(solution)/shard_map/ppermute | solution.py:21
  206.8 16.5 %collective-permute-start.19 = (f32[1,4,1,1024]{3,0,2,1:T(1,128)S(1)}, f32[1,4,1,1024]{3,0,2,1:T(1,128)S(1)}, u32[]{:S(2)}, u32[]{:S(2)}) collective-permute-start(f32[1,4,1,1024]{3,0,2,1:T(1,128)S(1)} %get-tuple-element.104), channel_id=1, source_target_pairs={{0,1},{1,2},{2,3},{3,4},{4,5},{5,6},{6,7},{8,9},{9,10},{10,11},{11... | collective-permute-start | bytes 49160 | tf_op jit(solution)/shard_map/ppermute | solution.py:18
  225.0 17.3 %collective-permute-start.20 = (f32[1,4,1,1024]{3,0,2,1:T(1,128)S(1)}, f32[1,4,1,1024]{3,0,2,1:T(1,128)S(1)}, u32[]{:S(2)}, u32[]{:S(2)}) collective-permute-start(f32[1,4,1,1024]{3,0,2,1:T(1,128)S(1)} %get-tuple-element.99), channel_id=1, source_target_pairs={{1,0},{2,1},{3,2},{4,3},{5,4},{6,5},{7,6},{9,8},{10,9},{11,10},{12... | collective-permute-start | bytes 49160 | tf_op jit(solution)/shard_map/ppermute | solution.py:21
  227.0 16.5 %collective-permute-start.21 = (f32[1,4,1,1024]{3,0,2,1:T(1,128)S(1)}, f32[1,4,1,1024]{3,0,2,1:T(1,128)S(1)}, u32[]{:S(2)}, u32[]{:S(2)}) collective-permute-start(f32[1,4,1,1024]{3,0,2,1:T(1,128)S(1)} %get-tuple-element.100), channel_id=1, source_target_pairs={{0,1},{1,2},{2,3},{3,4},{4,5},{5,6},{6,7},{8,9},{9,10},{10,11},{11... | collective-permute-start | bytes 49160 | tf_op jit(solution)/shard_map/ppermute | solution.py:18
  245.2 17.3 %collective-permute-start.22 = (f32[1,4,1,1024]{3,0,2,1:T(1,128)S(1)}, f32[1,4,1,1024]{3,0,2,1:T(1,128)S(1)}, u32[]{:S(2)}, u32[]{:S(2)}) collective-permute-start(f32[1,4,1,1024]{3,0,2,1:T(1,128)S(1)} %get-tuple-element.95), channel_id=1, source_target_pairs={{1,0},{2,1},{3,2},{4,3},{5,4},{6,5},{7,6},{9,8},{10,9},{11,10},{12... | collective-permute-start | bytes 49160 | tf_op jit(solution)/shard_map/ppermute | solution.py:21
  247.1 16.5 %collective-permute-start.23 = (f32[1,4,1,1024]{3,0,2,1:T(1,128)S(1)}, f32[1,4,1,1024]{3,0,2,1:T(1,128)S(1)}, u32[]{:S(2)}, u32[]{:S(2)}) collective-permute-start(f32[1,4,1,1024]{3,0,2,1:T(1,128)S(1)} %get-tuple-element.96), channel_id=1, source_target_pairs={{0,1},{1,2},{2,3},{3,4},{4,5},{5,6},{6,7},{8,9},{9,10},{10,11},{11... | collective-permute-start | bytes 49160 | tf_op jit(solution)/shard_map/ppermute | solution.py:18
  265.4 17.4 %collective-permute-start.24 = (f32[1,4,1,1024]{3,0,2,1:T(1,128)S(1)}, f32[1,4,1,1024]{3,0,2,1:T(1,128)S(1)}, u32[]{:S(2)}, u32[]{:S(2)}) collective-permute-start(f32[1,4,1,1024]{3,0,2,1:T(1,128)S(1)} %get-tuple-element.91), channel_id=1, source_target_pairs={{1,0},{2,1},{3,2},{4,3},{5,4},{6,5},{7,6},{9,8},{10,9},{11,10},{12... | collective-permute-start | bytes 49160 | tf_op jit(solution)/shard_map/ppermute | solution.py:21
  267.3 16.5 %collective-permute-start.25 = (f32[1,4,1,1024]{3,0,2,1:T(1,128)S(1)}, f32[1,4,1,1024]{3,0,2,1:T(1,128)S(1)}, u32[]{:S(2)}, u32[]{:S(2)}) collective-permute-start(f32[1,4,1,1024]{3,0,2,1:T(1,128)S(1)} %get-tuple-element.92), channel_id=1, source_target_pairs={{0,1},{1,2},{2,3},{3,4},{4,5},{5,6},{6,7},{8,9},{9,10},{10,11},{11... | collective-permute-start | bytes 49160 | tf_op jit(solution)/shard_map/ppermute | solution.py:18
  285.6 17.3 %collective-permute-start.26 = (f32[1,4,1,1024]{3,0,2,1:T(1,128)S(1)}, f32[1,4,1,1024]{3,0,2,1:T(1,128)S(1)}, u32[]{:S(2)}, u32[]{:S(2)}) collective-permute-start(f32[1,4,1,1024]{3,0,2,1:T(1,128)S(1)} %get-tuple-element.87), channel_id=1, source_target_pairs={{1,0},{2,1},{3,2},{4,3},{5,4},{6,5},{7,6},{9,8},{10,9},{11,10},{12... | collective-permute-start | bytes 49160 | tf_op jit(solution)/shard_map/ppermute | solution.py:21
  287.5 16.5 %collective-permute-start.27 = (f32[1,4,1,1024]{3,0,2,1:T(1,128)S(1)}, f32[1,4,1,1024]{3,0,2,1:T(1,128)S(1)}, u32[]{:S(2)}, u32[]{:S(2)}) collective-permute-start(f32[1,4,1,1024]{3,0,2,1:T(1,128)S(1)} %get-tuple-element.88), channel_id=1, source_target_pairs={{0,1},{1,2},{2,3},{3,4},{4,5},{5,6},{6,7},{8,9},{9,10},{10,11},{11... | collective-permute-start | bytes 49160 | tf_op jit(solution)/shard_map/ppermute | solution.py:18
Sparse Core Ops, SparseCore 0:
  320.9 461.7 reduce-scatter.3
